TPU v7x, 1024 devices: a whole 8x8x8 slice. The times are simulated.
1024 devices in a mesh: grp: 16 (over y, core), emb: 64 (over x, z).
Axes of the slice: x: 8, y: 8, z: 8, core: 2. Of those that a mesh axis runs over, the one named last changes fastest.
Arguments:
- table_window: bfloat16 [131072, 128], P('emb'), may hold values from -3 to 3
- dense_part: bfloat16 [131072, 128], P(('grp', 'emb')), may hold values from -6 to 6
- bag_rows: int32 [131072, 26, 8], P(('grp', 'emb')), may hold values from 0 to 2047
- bag_lengths: int32 [131072, 26], P(('grp', 'emb')), may hold values from 1 to 8
- bag_owner: int32 [131072, 26, 1], P(('grp', 'emb')), may hold values from 0 to 63; in each aligned block of 3328 rows (0 to 3327, 3328 to 6655, ..., all dimensions but the last counted through in order) at most 78 rows name the same one
- labels: int32 [131072], P(('grp', 'emb')), may hold values 0 or 1
- sample_weight: float32 [131072], P(('grp', 'emb')), may hold values from 0.005 to 1.5
- down_w: bfloat16 [3456, 512], replicated, may hold values from -0.109375 to 0.109375
- up_w: bfloat16 [512, 3456], replicated, may hold values from -0.25 to 0.25
- cross_bias: float32 [3456], replicated, may hold values from -3 to 3
- head_w: float32 [3456], replicated, may hold values from -0.109375 to 0.109375
Outputs:
- row_grad: float32 [131072, 128], P('emb')
- head_grad: float32 [3456], replicated
- bias_grad: float32 [3456], replicated
- dense_grad: bfloat16 [131072, 128], P(('grp', 'emb'))
Inputs may be any that keep to these rules, and one draw needn't show every extreme that they name: `bag_owner`: among the bags of the samples of one device (aligned blocks of 128 samples), at most 78 have one owner, and some owner has exactly 78.
All inputs are finite; a program needn't handle non-finite values. No bound on the sum of `labels` on one device may be relied on, other than what follows from the above.
Results may differ from a plain program's by a relative error of at most 0.0045.
The roundings to bfloat16 on the way count: a program that leaves them out, or rounds other values in their place, can miss the bound.
Values may be sent and summed in bfloat16 or wider, within the bound.
A program may use at most 128 MiB of HBM per device.

v0:
```python
import jax
import jax.numpy as jnp
from jax import lax
from jax.sharding import PartitionSpec as P


def body(
    table_window,
    dense_part,
    bag_rows,
    bag_lengths,
    bag_owner,
    labels,
    sample_weight,
    down_w,
    up_w,
    cross_bias,
    head_w,
):
    owners = lax.axis_size("emb")
    samples = dense_part.shape[0]
    width = dense_part.shape[1]
    tables = bag_rows.shape[1]
    hot = bag_rows.shape[2]
    local_rows = table_window.shape[0]
    bags = samples * tables
    capacity = bags * 3 // (2 * owners)
    owner = bag_owner.reshape(bags)
    owner_hits = (owner[:, None] == jnp.arange(owners, dtype=jnp.int32)[None, :]).astype(jnp.int32)
    ranks = jnp.cumsum(owner_hits, axis=0) - 1
    slot = jnp.sum(ranks * owner_hits, axis=1)
    position = owner * capacity + slot
    live = jnp.arange(hot, dtype=jnp.int32)[None, None, :] < bag_lengths[:, :, None]
    entries = jnp.where(live, bag_rows, -1).reshape(bags, hot)
    requests = jnp.full((owners * capacity, hot), -1, jnp.int32).at[position].set(entries)
    requests = requests.reshape(owners, capacity, hot)
    received = lax.all_to_all(requests, "emb", split_axis=0, concat_axis=0, tiled=True)
    count = received.shape[1]
    flat = received.reshape(owners * count, hot)
    summed = jnp.zeros((owners * count, width), jnp.float32)
    for pool_entry in range(hot):
        pool_index = flat[:, pool_entry]
        pool_valid = pool_index >= 0
        picked = table_window[jnp.where(pool_valid, pool_index, 0)].astype(jnp.float32)
        summed = summed + jnp.where(pool_valid[:, None], picked, 0.0)
    returned = lax.all_to_all(
        summed.astype(jnp.bfloat16).reshape(owners, count, width),
        "emb",
        split_axis=0,
        concat_axis=0,
        tiled=True,
    )
    pooled = returned.reshape(owners * capacity, width)[position].reshape(samples, tables * width)
    x0 = jnp.concatenate([dense_part, pooled], axis=1)
    low = jnp.dot(x0, down_w, preferred_element_type=jnp.float32).astype(jnp.bfloat16)
    cross = jnp.dot(low, up_w, preferred_element_type=jnp.float32) + cross_bias[None, :]
    x0f = x0.astype(jnp.float32)
    x1 = x0f * cross + x0f
    logit = jnp.dot(x1, head_w, precision=lax.Precision.HIGHEST)
    dlogit = sample_weight * (jax.nn.sigmoid(logit) - labels.astype(jnp.float32))
    d_x1 = dlogit[:, None] * head_w[None, :]
    head_part = jnp.dot(dlogit, x1, precision=lax.Precision.HIGHEST)
    bias_part = jnp.sum(d_x1 * x0f, axis=0)
    d_cross = (d_x1 * x0f).astype(jnp.bfloat16)
    d_low = jnp.dot(d_cross, up_w.T, preferred_element_type=jnp.float32).astype(jnp.bfloat16)
    d_x0 = d_x1 * (cross + 1.0) + jnp.dot(d_low, down_w.T, preferred_element_type=jnp.float32)
    dense_grad = d_x0[:, :width].astype(jnp.bfloat16)
    d_pooled = d_x0[:, width:].astype(jnp.bfloat16).reshape(bags, width)
    outgoing = jnp.zeros((owners * capacity, width), jnp.bfloat16).at[position].set(d_pooled)
    incoming = lax.all_to_all(
        outgoing.reshape(owners, capacity, width), "emb", split_axis=0, concat_axis=0, tiled=True
    )
    incoming_f = incoming.reshape(owners * capacity, width).astype(jnp.float32)
    held_flat = received.reshape(owners * capacity, hot)
    row_part = jnp.zeros((local_rows, width), jnp.float32)
    for entry in range(hot):
        index = held_flat[:, entry]
        valid = index >= 0
        row_part = row_part.at[jnp.where(valid, index, 0)].add(
            jnp.where(valid[:, None], incoming_f, 0.0)
        )
    row_grad = lax.psum(row_part, "grp")
    head_grad, bias_grad = lax.psum((head_part, bias_part), ("grp", "emb"))
    return (row_grad, head_grad, bias_grad, dense_grad)


def solution(mesh):
    in_specs = (
        P("emb", None),
        P(("grp", "emb"), None),
        P(("grp", "emb"), None, None),
        P(("grp", "emb"), None),
        P(("grp", "emb"), None, None),
        P(("grp", "emb")),
        P(("grp", "emb")),
        P(),
        P(),
        P(),
        P(),
    )
    out_specs = (P("emb", None), P(), P(), P(("grp", "emb"), None))
    return jax.shard_map(body, mesh=mesh, in_specs=in_specs, out_specs=out_specs, check_vma=False)
```

profile of v0, /device:TPU:1, one launch (start us, length us, event | category | flops | bytes accessed | tf_op | source)
XLA Modules:
  0.0 850.0 jit_solution(11689854492355452665)
XLA Ops:
  14.5 35.1 %reduce-window.6 = s32[64,26,128]{2,1,0:T(8,128)} reduce-window(s32[64,26,128]{2,1,0:T(8,128)} %fusion.47, s32[]{:T(128)} %constant.11.clone.1), window={size=1x1x128 pad=0_0x0_0x127_0}, to_apply=%region_0.0 | reduce-window | flops 27049984 | bytes 1703940 | tf_op jit(solution)/shard_map/reduce-window
  72.1 15.1 %scatter_custom_fusion = s32[4992,8]{1,0:T(8,128)} fusion(s32[3328]{0:T(1024)S(1)} %fusion.69, s32[3328,8]{1,0:T(8,128)} %copy.36, s32[]{:T(128)} %constant.9.clone.1), kind=kCustom, calls=%fused_computation.52 | custom fusion | bytes 160256 | tf_op jit(solution)/shard_map/scatter | solution.py:35
  87.2 3.1 copy.37
  93.3 35.7 %all_to_all.15 = s32[64,78,8]{1,2,0:T(8,128)S(1)} all-to-all(s32[64,78,8]{1,2,0:T(8,128)S(1)} %copy.38), channel_id=1, replica_groups=mesh['grp'=16,'emb'=64] {'emb'}, dimensions={0} | all-to-all | bytes 319488 | tf_op jit(solution)/shard_map/all_to_all | solution.py:37
  138.1 12.2 %gather_fusion = bf16[4992,128]{1,0:T(8,128)(2,1)} fusion(bf16[2048,128]{1,0:T(8,128)(2,1)} %param.11, s32[5120]{0:T(1024)} %get-tuple-element.29), kind=kCustom, calls=%fused_computation | custom fusion | bytes 2575872 | tf_op jit(solution)/shard_map/gather | solution.py:44
  153.3 12.2 %gather_fusion.1 = bf16[4992,128]{1,0:T(8,128)(2,1)} fusion(bf16[2048,128]{1,0:T(8,128)(2,1)} %param.11, s32[5120]{0:T(1024)} %get-tuple-element.28), kind=kCustom, calls=%fused_computation.1 | custom fusion | bytes 2575872 | tf_op jit(solution)/shard_map/gather | solution.py:44
  169.8 12.2 %gather_fusion.2 = bf16[4992,128]{1,0:T(8,128)(2,1)} fusion(bf16[2048,128]{1,0:T(8,128)(2,1)} %param.11, s32[5120]{0:T(1024)} %get-tuple-element.27), kind=kCustom, calls=%fused_computation.2 | custom fusion | bytes 2575872 | tf_op jit(solution)/shard_map/gather | solution.py:44
  185.0 12.2 %gather_fusion.3 = bf16[4992,128]{1,0:T(8,128)(2,1)} fusion(bf16[2048,128]{1,0:T(8,128)(2,1)} %param.11, s32[5120]{0:T(1024)} %get-tuple-element.26), kind=kCustom, calls=%fused_computation.3 | custom fusion | bytes 2575872 | tf_op jit(solution)/shard_map/gather | solution.py:44
  197.2 3.1 reshape.161
  201.6 12.2 %gather_fusion.4 = bf16[4992,128]{1,0:T(8,128)(2,1)} fusion(bf16[2048,128]{1,0:T(8,128)(2,1)} %param.11, s32[5120]{0:T(1024)} %get-tuple-element.25), kind=kCustom, calls=%fused_computation.4 | custom fusion | bytes 2575872 | tf_op jit(solution)/shard_map/gather | solution.py:44
  216.8 12.2 %gather_fusion.5 = bf16[4992,128]{1,0:T(8,128)(2,1)} fusion(bf16[2048,128]{1,0:T(8,128)(2,1)} %param.11, s32[5120]{0:T(1024)} %get-tuple-element.24), kind=kCustom, calls=%fused_computation.5 | custom fusion | bytes 2575872 | tf_op jit(solution)/shard_map/gather | solution.py:44
  233.3 12.2 %gather_fusion.6 = bf16[4992,128]{1,0:T(8,128)(2,1)} fusion(bf16[2048,128]{1,0:T(8,128)(2,1)} %param.11, s32[5120]{0:T(1024)} %get-tuple-element.23), kind=kCustom, calls=%fused_computation.6 | custom fusion | bytes 2575872 | tf_op jit(solution)/shard_map/gather | solution.py:44
  248.5 12.2 %gather_fusion.7 = bf16[4992,128]{1,0:T(8,128)(2,1)} fusion(bf16[2048,128]{1,0:T(8,128)(2,1)} %param.11, s32[5120]{0:T(1024)} %get-tuple-element.22), kind=kCustom, calls=%fused_computation.7 | custom fusion | bytes 2575872 | tf_op jit(solution)/shard_map/gather | solution.py:44
  273.3 12.7 %add_convert_fusion = bf16[64,78,128]{2,1,0:T(8,128)(2,1)} fusion(f32[64,78,128]{2,1,0:T(8,128)} %reshape.165, f32[64,78,128]{2,1,0:T(8,128)} %reshape.164, f32[64,78,128]{2,1,0:T(8,128)} %reshape.163, f32[64,78,128]{2,1,0:T(8,128)} %reshape.162, f32[64,78,128]{2,1,0:T(8,128)} %reshape.161, f32[64,78,128]{2,1,0:T(8,128)} %reshape.160, ...), kind=kLoop, calls=%fused_computation.23 | loop fusion | flops 10223616 | bytes 21765120 | tf_op jit(solution)/shard_map/convert_element_type | solution.py:47
  285.9 6.7 all-to-all-start.1
  296.3 27.6 %all-to-all-done.1 = bf16[64,78,128]{2,1,0:T(8,128)(2,1)} async-done(((bf16[64,78,128]{2,1,0:T(8,128)(2,1)}), bf16[64,78,128]{2,1,0:T(8,128)(2,1)}, u32[]{:S(2)}, u32[]{:S(2)}) %all-to-all-start.1) | async-done | bytes 1277984 | tf_op jit(solution)/shard_map/all_to_all | solution.py:46
  326.9 9.2 %gather_fusion.8 = bf16[3328,128]{1,0:T(8,128)(2,1)} fusion(bf16[4992,128]{1,0:T(8,128)(2,1)} %reshape.154, s32[4096]{0:T(1024)} %pad_clamp_fusion.8), kind=kCustom, calls=%fused_computation.8 | custom fusion | bytes 1717248 | tf_op jit(solution)/shard_map/gather | solution.py:53
  341.0 4.7 convolution_add_fusion.1
  345.7 3.9 fusion.46
  349.6 6.1 fusion
  360.7 14.9 %scatter_custom_fusion.1 = bf16[4992,128]{1,0:T(8,128)(2,1)} fusion(s32[3328]{0:T(1024)} %copy-done.5, bf16[3328,128]{1,0:T(8,128)(2,1)} %reshape.251, bf16[]{:T(256)} %constant.14.clone.1), kind=kCustom, calls=%fused_computation.83 | custom fusion | bytes 1278464 | tf_op jit(solution)/shard_map/scatter | solution.py:69
  378.5 41.7 %all_to_all.16 = bf16[64,78,128]{2,1,0:T(8,128)(2,1)} all-to-all(bf16[64,78,128]{2,1,0:T(8,128)(2,1)} %reshape.157), channel_id=1, replica_groups=mesh['grp'=16,'emb'=64] {'emb'}, dimensions={0} | all-to-all | bytes 2555904 | tf_op jit(solution)/shard_map/all_to_all | solution.py:70
  423.2 29.3 %scatter_custom_fusion.2 = f32[2048,128]{1,0:T(8,128)} fusion(s32[4992]{0:T(1024)} %copy-done.3, f32[4992,128]{1,0:T(8,128)} %reshape.166, f32[]{:T(128)} %constant.8.clone.1, pred[4992]{0:T(1024)(128)(4,1)} %get-tuple-element.4), kind=kCustom, calls=%fused_computation.38 | custom fusion | flops 1277952 | bytes 3610624 | tf_op jit(solution)/shard_map/scatter-add | solution.py:79
  452.5 30.5 %scatter_custom_fusion.3 = f32[2048,128]{1,0:T(8,128)} fusion(f32[2048,128]{1,0:T(8,128)} %scatter_custom_fusion.2, s32[4992]{0:T(1024)} %copy-done.2, f32[4992,128]{1,0:T(8,128)} %reshape.166, f32[]{:T(128)} %constant.8.clone.1, pred[4992]{0:T(1024)(128)(4,1)} %get-tuple-element.11), kind=kCustom, calls=%fused_computation.36 | custom fusion | flops 1277952 | bytes 3610112 | tf_op jit(solution)/shard_map/scatter-add | solution.py:79
  483.0 30.5 %scatter_custom_fusion.4 = f32[2048,128]{1,0:T(8,128)} fusion(f32[2048,128]{1,0:T(8,128)} %scatter_custom_fusion.3, s32[4992]{0:T(1024)} %get-tuple-element.14, f32[4992,128]{1,0:T(8,128)} %reshape.166, f32[]{:T(128)} %constant.8.clone.1, pred[4992]{0:T(1024)(128)(4,1)} %get-tuple-element.10), kind=kCustom, calls=%fused_computation.34 | custom fusion | flops 1277952 | bytes 3610112 | tf_op jit(solution)/shard_map/scatter-add | solution.py:79
  513.6 30.7 %scatter_custom_fusion.5 = f32[2048,128]{1,0:T(8,128)} fusion(f32[2048,128]{1,0:T(8,128)} %scatter_custom_fusion.4, s32[4992]{0:T(1024)} %get-tuple-element.15, f32[4992,128]{1,0:T(8,128)} %reshape.166, f32[]{:T(128)} %constant.8.clone.1, pred[4992]{0:T(1024)(128)(4,1)} %get-tuple-element.9), kind=kCustom, calls=%fused_computation.32 | custom fusion | flops 1277952 | bytes 3610112 | tf_op jit(solution)/shard_map/scatter-add | solution.py:79
  544.2 30.6 %scatter_custom_fusion.6 = f32[2048,128]{1,0:T(8,128)} fusion(f32[2048,128]{1,0:T(8,128)} %scatter_custom_fusion.5, s32[4992]{0:T(1024)} %get-tuple-element.16, f32[4992,128]{1,0:T(8,128)} %reshape.166, f32[]{:T(128)} %constant.8.clone.1, pred[4992]{0:T(1024)(128)(4,1)} %get-tuple-element.8), kind=kCustom, calls=%fused_computation.30 | custom fusion | flops 1277952 | bytes 3610112 | tf_op jit(solution)/shard_map/scatter-add | solution.py:79
  574.9 31.0 %scatter_custom_fusion.7 = f32[2048,128]{1,0:T(8,128)} fusion(f32[2048,128]{1,0:T(8,128)} %scatter_custom_fusion.6, s32[4992]{0:T(1024)} %get-tuple-element.17, f32[4992,128]{1,0:T(8,128)} %reshape.166, f32[]{:T(128)} %constant.8.clone.1, pred[4992]{0:T(1024)(128)(4,1)} %get-tuple-element.7), kind=kCustom, calls=%fused_computation.28 | custom fusion | flops 1277952 | bytes 3610112 | tf_op jit(solution)/shard_map/scatter-add | solution.py:79
  605.8 32.9 %scatter_custom_fusion.8 = f32[2048,128]{1,0:T(8,128)} fusion(f32[2048,128]{1,0:T(8,128)} %scatter_custom_fusion.7, s32[4992]{0:T(1024)} %get-tuple-element.18, f32[4992,128]{1,0:T(8,128)} %reshape.166, f32[]{:T(128)} %constant.8.clone.1, pred[4992]{0:T(1024)(128)(4,1)} %copy-done.7), kind=kCustom, calls=%fused_computation.26 | custom fusion | flops 1277952 | bytes 3610112 | tf_op jit(solution)/shard_map/scatter-add | solution.py:79
  638.7 36.7 %scatter_custom_fusion.9 = f32[2048,128]{1,0:T(8,128)} fusion(f32[2048,128]{1,0:T(8,128)} %scatter_custom_fusion.8, s32[4992]{0:T(1024)} %get-tuple-element.19, f32[4992,128]{1,0:T(8,128)} %reshape.166, f32[]{:T(128)} %constant.8.clone.1, pred[4992]{0:T(1024)(128)(4,1)} %copy-done.6), kind=kCustom, calls=%fused_computation.24 | custom fusion | flops 1277952 | bytes 3610112 | tf_op jit(solution)/shard_map/scatter-add | solution.py:79
  678.9 3.4 fusion.39
  682.4 158.3 %all-reduce = (f32[3456]{0:T(1024)}, f32[3456]{0:T(1024)}) all-reduce(f32[3456]{0:T(1024)} %fusion.39, f32[3456]{0:T(1024)S(1)} %copy-done.4), channel_id=1, replica_groups=mesh['grp'=16,'emb'=64] {'grp','emb'}, use_global_device_ids=true, to_apply=%region_14.15 | all-reduce | flops 6912 | bytes 55296 | tf_op jit(solution)/shard_map/psum | solution.py:83
  (74 shorter events, 104.8 us)
Async XLA Ops:
  7.2 333.8 %copy-start = (bf16[3456,512]{1,0:T(8,128)(2,1)S(1)}, bf16[3456,512]{1,0:T(8,128)(2,1)}, u32[]{:S(2)}) copy-start(bf16[3456,512]{1,0:T(8,128)(2,1)} %param.18) | copy-start | bytes 10616836
  72.1 18.2 %copy-start.5 = (s32[3328]{0:T(1024)}, s32[3328]{0:T(1024)S(1)}, u32[]{:S(2)}) copy-start(s32[3328]{0:T(1024)S(1)} %fusion.69) | copy-start | bytes 39940
  134.5 2.9 copy-start.2
  134.5 3.6 copy-start.3
  137.5 134.9 %copy-start.7 = (pred[4992]{0:T(1024)(128)(4,1)}, pred[4992]{0:T(1024)(128)(4,1)S(1)}, u32[]{:S(2)}) copy-start(pred[4992]{0:T(1024)(128)(4,1)S(1)} %get-tuple-element.6) | copy-start | bytes 14980
  137.5 135.6 %copy-start.6 = (pred[4992]{0:T(1024)(128)(4,1)}, pred[4992]{0:T(1024)(128)(4,1)S(1)}, u32[]{:S(2)}) copy-start(pred[4992]{0:T(1024)(128)(4,1)S(1)} %get-tuple-element.5) | copy-start | bytes 14980
  285.9 7.0 copy-start.1
  285.9 37.9 %all-to-all-start.1 = ((bf16[64,78,128]{2,1,0:T(8,128)(2,1)}), bf16[64,78,128]{2,1,0:T(8,128)(2,1)}, u32[]{:S(2)}, u32[]{:S(2)}) async-start(bf16[64,78,128]{2,1,0:T(8,128)(2,1)} %add_convert_fusion), calls=%async_computation.1 | async-start | bytes 2621440 | tf_op jit(solution)/shard_map/all_to_all | solution.py:46
  292.7 547.9 %all-reduce.3.cloned.1.call-start = ((), (), s32[]{:S(2)}) async-start(), calls=%async_computation.3 | async-start | bytes 2097152 | tf_op jit(solution)/shard_map/psum | solution.py:82
  678.9 3.4 copy-start.4
Sparse Core Ops, SparseCore 0:
  675.6 163.0 all-reduce.2
where the time goes:
time: 865 us; the launch traced here: 850 us
  other arithmetic  325 us (38%)
  blocking collectives  236 us (27%)
  local copies, waits for them, and re-layouts  222 us (26%)
  waiting for transfers between devices  27.6 us (3%)
  matrix products  18.1 us (2%)
  between operations  14.4 us (2%)
    scatter-add x8, other arithmetic, body(): row_part.at[jnp.where(valid, index, 0)]  252 us
    psum x1, blocking collectives, body(): head_grad, bias_grad = lax.psum((head_part, bias_part), ('grp', 'emb'))  158 us
    gather x8, local copies, waits for them, and re-layouts, body(): table_window[jnp.where(pool_valid, pool_index, 0)].astype(jnp.float32)  97.4 us
    all_to_all x1, blocking collectives, body(): lax.all_to_all(outgoing.reshape(owners, capacity, width), 'emb', split_ax...  41.7 us
    another operation x2, other arithmetic  36.7 us
    all_to_all x1, blocking collectives, body(): lax.all_to_all(requests, 'emb', split_axis=0, concat_axis=0, tiled=True)  35.7 us
    all_to_all x1, waiting for transfers between devices, body(): lax.all_to_all(summed.astype(jnp.bfloat16).reshape(owners, count, width),...  27.6 us
    convert_element_type x8, local copies, waits for them, and re-layouts, body(): table_window[jnp.where(pool_valid, pool_index, 0)].astype(jnp.float32)  24.2 us
  transfers between devices with their start and end apart: 2, of which 1 were waited for; matrix products, arithmetic and copies ran while one was open for 1% of the time, Pallas kernels for 0%

commit v1 on v0

v1 whole, which is shorter than its diff:
```python
import functools

import jax
import jax.numpy as jnp
from jax import lax
from jax.experimental import pallas as pl
from jax.experimental.pallas import tpu as pltpu
from jax.sharding import PartitionSpec as P

MESH = pl.DeviceIdType.MESH
F32 = jnp.float32
BF16 = jnp.bfloat16
I32 = jnp.int32
NT = (((1,), (1,)), ((), ()))
LAG = 2


def iota(shape, dim):
    return lax.broadcasted_iota(I32, shape, dim)


def hot(mask):
    return jnp.where(mask, 1.0, 0.0).astype(BF16)


def kernel(
    ring, tables, slots, pairs,
    own_ref, len_ref, rows_ref, label_ref, weight_ref, dense_ref, table_ref, bias_ref, head_ref,
    down_any, up_any,
    rg_ref, hb_ref, dg_ref,
    down, up, pos_row, pos_col, req_acc, code_s, code_r, counts, pool_s, pool_r, grad_s, grad_r,
    x0, x0_acc, cross, d_pool, chunk_acc, acc, pair_r, rs_r,
    hb, h1, h2, h3, h4,
    w_sem, code_ss, code_rs, pool_ss, pool_rs, grad_ss, grad_rs,
    pr_ss, pr_rs, rs_ss, rs_rs, ag_ss, ag_rs, pa_ss, pa_rs, h_ss, h_rs,
):
    peers = ring * ring
    groups = 2 * pairs
    chunk = ring * slots
    bits = ring.bit_length() - 1
    code_rows = slots * 8 // 128
    local_rows, width = table_ref.shape
    block = local_rows // groups
    tiles = tables + 1
    me = lax.axis_index("emb")
    grp = lax.axis_index("grp")
    x, z = me // ring, lax.rem(me, ring)
    y, c = grp // 2, lax.rem(grp, 2)
    mate = {"grp": grp + 1 - 2 * c}

    def ahead(k):
        dx = lax.rem(k, ring)
        dz = lax.rem(dx + k // ring, ring)
        return {"emb": lax.rem(x + dx, ring) * ring + lax.rem(z + dz, ring)}

    def behind(k):
        dx = lax.rem(k, ring)
        dz = lax.rem(dx + k // ring, ring)
        return {"emb": lax.rem(x + ring - dx, ring) * ring + lax.rem(z + ring - dz, ring)}

    def along_x(d):
        return {"emb": lax.rem(x + d, ring) * ring + z}

    def along_z(d):
        return {"emb": x * ring + lax.rem(z + d, ring)}

    def along_y(d):
        return {"grp": lax.rem(y + d, pairs) * 2 + c}

    def remote(src, dst, send, recv, where):
        return pltpu.make_async_remote_copy(
            src_ref=src, dst_ref=dst, send_sem=send, recv_sem=recv, device_id=where, device_id_type=MESH
        )

    def loop(low, high, step):
        def run(i, carry):
            step(i)
            return carry

        lax.fori_loop(low, high, run, 0)

    down_copy = pltpu.make_async_copy(down_any, down, w_sem.at[0])
    up_copy = pltpu.make_async_copy(up_any, up, w_sem.at[1])
    down_copy.start()
    up_copy.start()

    barrier = pltpu.get_barrier_semaphore()
    loop(1, peers, lambda k: pl.semaphore_signal(barrier, inc=1, device_id=ahead(k), device_id_type=MESH))
    loop(1, pairs, lambda d: pl.semaphore_signal(barrier, inc=1, device_id=along_y(d), device_id_type=MESH))
    pl.semaphore_signal(barrier, inc=1, device_id=mate, device_id_type=MESH)

    req_acc[...] = jnp.zeros_like(req_acc)
    upper = jnp.concatenate([hot(iota((128, 128), 0) < iota((128, 128), 1)), jnp.ones((128, 128), BF16)], axis=1)

    def bucket(t, carry):
        owner = own_ref[pl.ds(t, 1), :]
        dx = ((owner >> bits) - x) & (ring - 1)
        dz = ((owner & (ring - 1)) - z) & (ring - 1)
        kind = ((dz - dx) & (ring - 1)) * ring + dx
        mine = iota((128, 128), 0) == kind
        mine_f = jnp.where(mine, 1.0, 0.0)
        sums = jnp.dot(mine_f.astype(BF16), upper, preferred_element_type=F32)
        slot = jnp.sum(mine_f * (sums[:, :128] + carry), axis=0, keepdims=True).astype(I32)
        pos_row[pl.ds(t, 1), :] = kind * slots + slot
        live = iota((8, 128), 0) < len_ref[pl.ds(t, 1), :]
        code = jnp.where(live, rows_ref[pl.ds(pl.multiple_of(t * 8, 8), 8), :] + 1, 0)
        high = (code >> 4).astype(F32)
        low = (code & 15).astype(F32)
        here = [slot == s for s in range(slots)]
        spread = jnp.concatenate(
            [jnp.where(h, high, 0.0) for h in here] + [jnp.where(h, low, 0.0) for h in here], axis=0
        ).astype(BF16)
        req_acc[...] += lax.dot_general(spread, mine_f.astype(BF16), NT, preferred_element_type=F32)
        return carry + sums[:, 128:]

    lax.fori_loop(0, tables, bucket, jnp.zeros((128, 128), F32))
    for p in range(code_rows):
        high = req_acc[p * 128:(p + 1) * 128, :]
        low = req_acc[slots * 8 + p * 128:slots * 8 + (p + 1) * 128, :]
        tile = (high * 16.0 + low - 1.0).T
        code_s[pl.ds(p, peers, stride=8), :] = tile[:peers].astype(I32)

    pl.semaphore_wait(barrier, peers - 1 + pairs - 1 + 1)

    def code_copy(k):
        part = pl.ds(pl.multiple_of(k * 8, 8), 8)
        return remote(code_s.at[part], code_r.at[part], code_ss.at[k], code_rs.at[k], ahead(k))

    def pool_copy(k):
        part = pl.ds(pl.multiple_of(k * slots, 16), slots)
        return remote(pool_s.at[part], pool_r.at[part], pool_ss.at[k], pool_rs.at[k], behind(k))

    def grad_copy(k):
        part = pl.ds(pl.multiple_of(k * slots, 16), slots)
        return remote(grad_s.at[part], grad_r.at[part], grad_ss.at[k], grad_rs.at[k], ahead(k))

    loop(1, peers, lambda k: code_copy(k).start())
    code_r[0:8, :] = code_s[0:8, :]

    def turn(t):
        row = jnp.broadcast_to(pos_row[pl.ds(t, 1), :], (128, 128)).astype(F32)
        pos_col[pl.ds(pl.multiple_of(t * 128, 128), 128), :] = row.T.astype(I32)
        x0_acc[pl.ds(pl.multiple_of(t * 128, 128), 128), :] = jnp.zeros((128, 128), F32)

    loop(0, tables, turn)
    acc[...] = jnp.zeros_like(acc)

    def count_bags(k):
        tile = code_r[pl.ds(pl.multiple_of(k * 8, 8), 8), :]
        base = pl.multiple_of(k * slots, 16)
        for first in range(0, code_rows, 2):
            last = min(first + 2, code_rows)
            code = jnp.concatenate([tile[p:p + 1, :] for p in range(first, last)], axis=1)
            bags = (last - first) * 16
            lanes = bags * 8
            spans = local_rows // 256
            key = (code >> 8) * bags + (iota((1, lanes), 1) >> 3)
            left = hot(iota((spans * bags, lanes), 0) == key)
            right = hot(iota((256, lanes), 0) == (code & 255))
            out = lax.dot_general(left, right, NT, preferred_element_type=F32).astype(BF16)
            for s in range(spans):
                counts[pl.ds(base + first * 16, bags), s * 256:(s + 1) * 256] = out[s * bags:(s + 1) * bags, :]

    def pool_chunk(j):
        def one(i):
            k = j * ring + i

            @pl.when(k != 0)
            def _():
                code_copy(k).wait_recv()

            count_bags(k)

        loop(0, ring, one)
        part = pl.ds(pl.multiple_of(j * chunk, 16), chunk)
        pool_s[part, :] = jnp.dot(counts[part, :], table_ref[...], preferred_element_type=F32).astype(BF16)

        def send(i):
            k = j * ring + i

            @pl.when(k != 0)
            def _():
                pool_copy(k).start()

        loop(0, ring, send)

        @pl.when(j == 0)
        def _():
            pool_r[0:slots, :] = pool_s[0:slots, :]

    def place_chunk(j):
        def one(i):
            k = j * ring + i

            @pl.when(k != 0)
            def _():
                pool_copy(k).wait_recv()

        loop(0, ring, one)
        part = pl.ds(pl.multiple_of(j * chunk, 16), chunk)

        def some(t):
            rows = pl.ds(pl.multiple_of(t * 256, 256), 256)
            column = pos_col[rows, :] - j * chunk
            pick = jnp.concatenate([hot(column == iota((256, 128), 1) + q) for q in range(0, chunk, 128)], axis=1)
            x0_acc[rows, :] += jnp.dot(pick, pool_r[part, :], preferred_element_type=F32)

        loop(0, tables // 2, some)

    def forward(j):
        pool_chunk(j)

        @pl.when(j >= LAG)
        def _():
            place_chunk(j - LAG)

    loop(0, ring, forward)
    loop(ring - LAG, ring, place_chunk)

    down_copy.wait()
    up_copy.wait()
    x0[:, :width] = dense_ref[...]
    for t in range(tables):
        x0[:, (t + 1) * width:(t + 2) * width] = x0_acc[t * 128:(t + 1) * 128, :].astype(BF16)
    step = 3 * width
    cuts = range(0, tiles * width, step)
    low = jnp.zeros((128, down.shape[1]), F32)
    for a in cuts:
        low = low + jnp.dot(x0[:, a:a + step], down[a:a + step, :], preferred_element_type=F32)
    low = low.astype(BF16)
    logit_acc = jnp.zeros((128, width), F32)
    for a in cuts:
        part = jnp.dot(low, up[:, a:a + step], preferred_element_type=F32) + bias_ref[:, a:a + step]
        cross[:, a:a + step] = part
        x0f = x0[:, a:a + step].astype(F32)
        term = (x0f * part + x0f) * head_ref[:, a:a + step]
        for b in range(0, step, width):
            logit_acc = logit_acc + term[:, b:b + width]
    logit = jnp.sum(logit_acc, axis=1, keepdims=True)
    label = jnp.broadcast_to(label_ref[...].astype(F32), (128, 128)).T[:, 0:1]
    weight = jnp.broadcast_to(weight_ref[...], (128, 128)).T[:, 0:1]
    dlogit = weight * (jax.nn.sigmoid(logit) - label)
    hb[...] = jnp.zeros_like(hb)
    d_low = jnp.zeros((128, down.shape[1]), F32)
    for a in cuts:
        x0f = x0[:, a:a + step].astype(F32)
        x1 = x0f * cross[:, a:a + step] + x0f
        d_cross = dlogit * head_ref[:, a:a + step] * x0f
        head_part = jnp.sum(dlogit * x1, axis=0, keepdims=True)
        bias_part = jnp.sum(d_cross, axis=0, keepdims=True)
        for b in range(0, step, width):
            r = (a + b) // width
            hb[r:r + 1, :] = head_part[:, b:b + width]
            hb[tiles + r:tiles + r + 1, :] = bias_part[:, b:b + width]
        d_low = d_low + lax.dot_general(d_cross.astype(BF16), up[:, a:a + step], NT, preferred_element_type=F32)
    d_low = d_low.astype(BF16)

    def h_part(r):
        return pl.ds(pl.multiple_of(r * 8, 8), 8)

    def h1_copy(d):
        return remote(hb.at[h_part(lax.rem(x + d, ring))], h1.at[h_part(d)], h_ss.at[0, d], h_rs.at[0, d], along_x(d))

    def h2_copy(d):
        return remote(h2.at[h_part(z)], h2.at[h_part(z)], h_ss.at[1, d], h_rs.at[1, d], along_z(d))

    def h3_copy(d):
        return remote(h3.at[h_part(y)], h3.at[h_part(y)], h_ss.at[2, d], h_rs.at[2, d], along_y(d))

    def h4_copy():
        return remote(h4.at[h_part(c)], h4.at[h_part(c)], h_ss.at[3, 0], h_rs.at[3, 0], mate)

    def h5_copy(d):
        return remote(hb_ref.at[h_part(x)], hb_ref.at[h_part(x)], h_ss.at[4, d], h_rs.at[4, d], along_x(d))

    loop(1, ring, lambda d: h1_copy(d).start())

    def total_of(ref, count, start=0):
        total = ref[start * 8:start * 8 + 8, :]
        for r in range(start + 1, count):
            total = total + ref[r * 8:r * 8 + 8, :]
        return total

    def h_step1():
        loop(1, ring, lambda d: h1_copy(d).wait_recv())
        h2[h_part(z), :] = total_of(h1, ring, 1) + hb[h_part(x), :]
        loop(1, ring, lambda d: h2_copy(d).start())

    def h_step2():
        loop(1, ring, lambda d: h2_copy(d).wait_recv())
        h3[h_part(y), :] = total_of(h2, ring)
        loop(1, pairs, lambda d: h3_copy(d).start())

    def h_step3():
        loop(1, pairs, lambda d: h3_copy(d).wait_recv())
        h4[h_part(c), :] = total_of(h3, pairs)
        h4_copy().start()

    def h_step4():
        h4_copy().wait_recv()
        hb_ref[h_part(x), :] = total_of(h4, 2)
        loop(1, ring, lambda d: h5_copy(d).start())

    for a in cuts:
        d_x1 = dlogit * head_ref[:, a:a + step]
        d_x0 = d_x1 * (cross[:, a:a + step] + 1.0) + lax.dot_general(
            d_low, down[a:a + step, :], NT, preferred_element_type=F32
        )
        d_x0 = d_x0.astype(BF16)
        for b in range(0, step, width):
            t = (a + b) // width - 1
            if t < 0:
                dg_ref[...] = d_x0[:, b:b + width]
            else:
                d_pool[t * 128:(t + 1) * 128, :] = d_x0[:, b:b + width]

    def grad_chunk(j):
        chunk_acc[...] = jnp.zeros_like(chunk_acc)

        def some(t):
            rows = pl.ds(pl.multiple_of(t * 256, 256), 256)
            pick = jnp.concatenate(
                [
                    hot(iota((chunk, 128), 0) == pos_row[pl.ds(t * 2 + h, 1), :] - j * chunk)
                    for h in range(2)
                ],
                axis=1,
            )
            chunk_acc[...] += jnp.dot(pick, d_pool[rows, :], preferred_element_type=F32)

        loop(0, tables // 2, some)
        grad_s[pl.ds(pl.multiple_of(j * chunk, 16), chunk), :] = chunk_acc[...].astype(BF16)

        def send(i):
            k = j * ring + i

            @pl.when(k != 0)
            def _():
                grad_copy(k).start()

        loop(0, ring, send)

        @pl.when(j == 0)
        def _():
            grad_r[0:slots, :] = grad_s[0:slots, :]

    def row_chunk(j):
        def one(i):
            k = j * ring + i

            @pl.when(k != 0)
            def _():
                grad_copy(k).wait_recv()

        loop(0, ring, one)
        part = pl.ds(pl.multiple_of(j * chunk, 16), chunk)
        turned = grad_r[part, :].astype(F32).T.astype(BF16)
        for b in range(groups):
            acc[b] += jnp.dot(
                turned, counts[part, b * block:(b + 1) * block], preferred_element_type=F32
            )

    def backward(j):
        grad_chunk(j)

        @pl.when(j >= LAG)
        def _():
            row_chunk(j - LAG)

    loop(0, ring, backward)
    h_step1()
    h_step2()
    loop(ring - LAG, ring, row_chunk)

    def pr_copy(d):
        r = lax.rem(y + d, pairs)
        return remote(acc.at[(1 - c) * pairs + r], pair_r.at[r], pr_ss.at[d], pr_rs.at[d], mate)

    def rs_copy(d):
        return remote(pair_r.at[lax.rem(y + d, pairs)], rs_r.at[d], rs_ss.at[d], rs_rs.at[d], along_y(d))

    def out_block(side, r):
        return rg_ref.at[pl.ds(pl.multiple_of((side * pairs + r) * block, block), block)]

    def ag_copy(d):
        here = out_block(c, y)
        return remote(here, here, ag_ss.at[d], ag_rs.at[d], along_y(d))

    def pa_copy(d):
        here = out_block(c, lax.rem(y + pairs - d, pairs))
        return remote(here, here, pa_ss.at[d], pa_rs.at[d], mate)

    loop(0, pairs, lambda d: pr_copy(lax.rem(d + 1, pairs)).start())

    def pair_sum(n):
        d = lax.rem(n + 1, pairs)
        pr_copy(d).wait_recv()
        r = lax.rem(y + d, pairs)
        pair_r[r] = pair_r[r] + acc[c * pairs + r]

        @pl.when(d != 0)
        def _():
            rs_copy(d).start()

    loop(0, pairs, pair_sum)
    h_step3()
    loop(1, pairs, lambda d: rs_copy(d).wait_recv())
    total = pair_r[y]
    for d in range(1, pairs):
        total = total + rs_r[d]
    rg_ref[pl.ds(pl.multiple_of((c * pairs + y) * block, block), block), :] = total.T
    loop(1, pairs, lambda d: ag_copy(d).start())
    pa_copy(0).start()
    h_step4()

    def forward_block(d):
        ag_copy(d).wait_recv()
        pa_copy(d).start()

    loop(1, pairs, forward_block)
    loop(0, pairs, lambda d: pa_copy(d).wait_recv())
    loop(1, ring, lambda d: h5_copy(d).wait_recv())

    def sent(k):
        code_copy(k).wait_send()
        pool_copy(k).wait_send()
        grad_copy(k).wait_send()

    loop(1, peers, sent)

    def sent_x(d):
        h1_copy(d).wait_send()
        h2_copy(d).wait_send()
        h5_copy(d).wait_send()

    loop(1, ring, sent_x)

    def sent_y(d):
        h3_copy(d).wait_send()
        rs_copy(d).wait_send()
        ag_copy(d).wait_send()

    loop(1, pairs, sent_y)

    def sent_pair(d):
        pr_copy(d).wait_send()
        pa_copy(d).wait_send()

    loop(0, pairs, sent_pair)
    h4_copy().wait_send()


def body(
    table_window, dense_part, bag_rows, bag_lengths, bag_owner, labels, sample_weight, down_w, up_w, cross_bias, head_w
):
    peers = lax.axis_size("emb")
    groups = lax.axis_size("grp")
    ring = 1
    while ring * ring < peers:
        ring *= 2
    pairs = groups // 2
    samples, width = dense_part.shape
    tables, entries = bag_rows.shape[1:]
    local_rows = table_window.shape[0]
    cross_width, rank = down_w.shape
    capacity = samples * tables * 3 // (2 * peers)
    slots = -(-capacity // 16) * 16
    chunk = ring * slots
    bags = samples * tables
    block = local_rows // groups
    tiles = cross_width // width
    own = bag_owner.reshape(samples, tables).T
    lengths = bag_lengths.T
    rows = bag_rows.transpose(1, 2, 0).reshape(tables * entries, samples)
    vmem = pl.BlockSpec(memory_space=pltpu.VMEM)
    hbm = pl.BlockSpec(memory_space=pl.ANY)
    dma = pltpu.SemaphoreType.DMA
    row_grad, sums, dense_grad = pl.pallas_call(
        functools.partial(kernel, ring, tables, slots, pairs),
        out_shape=(
            jax.ShapeDtypeStruct((local_rows, width), F32),
            jax.ShapeDtypeStruct((ring * 8, width), F32),
            jax.ShapeDtypeStruct((samples, width), BF16),
        ),
        in_specs=[vmem] * 9 + [hbm] * 2,
        out_specs=(vmem, vmem, vmem),
        scratch_shapes=[
            pltpu.VMEM((cross_width, rank), BF16),
            pltpu.VMEM((rank, cross_width), BF16),
            pltpu.VMEM((-(-tables // 8) * 8, 128), I32),
            pltpu.VMEM((bags, 128), I32),
            pltpu.VMEM((2 * slots * 8, 128), F32),
            pltpu.VMEM((peers * 8, 128), I32),
            pltpu.VMEM((peers * 8, 128), I32),
            pltpu.VMEM((peers * slots, local_rows), BF16),
            pltpu.VMEM((peers * slots, width), BF16),
            pltpu.VMEM((peers * slots, width), BF16),
            pltpu.VMEM((peers * slots, width), BF16),
            pltpu.VMEM((peers * slots, width), BF16),
            pltpu.VMEM((samples, cross_width), BF16),
            pltpu.VMEM((bags, width), F32),
            pltpu.VMEM((samples, cross_width), F32),
            pltpu.VMEM((bags, width), BF16),
            pltpu.VMEM((chunk, width), F32),
            pltpu.VMEM((groups, width, block), F32),
            pltpu.VMEM((pairs, width, block), F32),
            pltpu.VMEM((pairs, width, block), F32),
            pltpu.VMEM((ring * 8, 128), F32),
            pltpu.VMEM((ring * 8, 128), F32),
            pltpu.VMEM((ring * 8, 128), F32),
            pltpu.VMEM((pairs * 8, 128), F32),
            pltpu.VMEM((16, 128), F32),
            dma((2,)),
            dma((peers,)),
            dma((peers,)),
            dma((peers,)),
            dma((peers,)),
            dma((peers,)),
            dma((peers,)),
            dma((pairs,)),
            dma((pairs,)),
            dma((pairs,)),
            dma((pairs,)),
            dma((pairs,)),
            dma((pairs,)),
            dma((pairs,)),
            dma((pairs,)),
            dma((5, max(ring, pairs))),
            dma((5, max(ring, pairs))),
        ],
        compiler_params=pltpu.CompilerParams(
            collective_id=0, has_side_effects=True, vmem_limit_bytes=60 * 1024 * 1024
        ),
    )(
        own, lengths, rows, labels.reshape(1, samples), sample_weight.reshape(1, samples), dense_part, table_window,
        cross_bias.reshape(1, cross_width), head_w.reshape(1, cross_width), down_w, up_w,
    )
    head_grad = sums[:tiles].reshape(cross_width)
    bias_grad = sums[tiles:2 * tiles].reshape(cross_width)
    return row_grad, head_grad, bias_grad, dense_grad


def solution(mesh):
    in_specs = (
        P("emb", None),
        P(("grp", "emb"), None),
        P(("grp", "emb"), None, None),
        P(("grp", "emb"), None),
        P(("grp", "emb"), None, None),
        P(("grp", "emb")),
        P(("grp", "emb")),
        P(),
        P(),
        P(),
        P(),
    )
    out_specs = (P("emb", None), P(), P(), P(("grp", "emb"), None))
    return jax.shard_map(body, mesh=mesh, in_specs=in_specs, out_specs=out_specs, check_vma=False)
```

time: 865 us -> 190 us (0.22); the launches traced: 850 us -> 189 us
  other arithmetic: 325 us -> 0 us
  blocking collectives: 236 us -> 0 us
  local copies, waits for them, and re-layouts: 222 us -> 9.01 us
  Pallas kernels: 0 us -> 179 us
  waiting for transfers between devices: 27.6 us -> 0 us
  matrix products: 18.1 us -> 0 us
  between operations: 14.4 us -> 0.64 us
    scatter-add x8 -> x0, other arithmetic: 252 us -> none  [body(): row_part.at[jnp.where(valid, index, 0)]]
    pallas_call x0 -> x1, Pallas kernels: none -> 179 us  [body(): pl.pallas_call(functools.partial(kernel, ring, tables, slots, pairs), out...]
    psum x1 -> x0, blocking collectives: 158 us -> none  [body(): head_grad, bias_grad = lax.psum((head_part, bias_part), ('grp', 'emb'))]
    gather x9 -> x0, local copies, waits for them, and re-layouts: 107 us -> none  [the longest x8 97.4 us: body(): table_window[jnp.where(pool_valid, pool_index, 0)].astype(jnp.float32)]
    all_to_all x2 -> x0, blocking collectives: 77.4 us -> none  [the longest x1 41.7 us: body(): lax.all_to_all(outgoing.reshape(owners, capacity, width), 'emb', split_ax...]
    another operation x2 -> x0, other arithmetic: 36.7 us -> none
    scatter x3 -> x0, local copies, waits for them, and re-layouts: 33 us -> none  [the longest x2 18.2 us: body(): jnp.full((owners * capacity, hot), -1, jnp.int32).at[position].set(entries)]
    all_to_all x1 -> x0, waiting for transfers between devices: 27.6 us -> none  [body(): lax.all_to_all(summed.astype(jnp.bfloat16).reshape(owners, count, width),...]
  transfers between devices with their start and end apart: 2 -> 0, of which waited for: 1 -> 0; matrix products, arithmetic and copies ran while one was open for 1% -> 0% of each run, Pallas kernels for 0% -> 0%
where the time goes in v1:
time: 190 us; the launch traced here: 189 us
  Pallas kernels  179 us (94%)
  local copies, waits for them, and re-layouts  9.01 us (5%)
    pallas_call x1, Pallas kernels, body(): pl.pallas_call(functools.partial(kernel, ring, tables, slots, pairs), out...  179 us
    unnamed x3, local copies, waits for them, and re-layouts  4.95 us

profile of v1, /device:TPU:1, one launch (start us, length us, event | category | flops | bytes accessed | tf_op | source)
XLA Modules:
  0.0 188.8 jit_solution(12214032752900833740)
XLA Ops:
  0.6 1.3 reshape.36.bias_ref
  2.0 1.3 reshape.37.head_ref
  3.3 1.3 copy.17
  4.6 179.2 %shard_map.138 = (f32[2048,128]{1,0:T(8,128)}, f32[64,128]{1,0:T(8,128)}, bf16[128,128]{1,0:T(8,128)(2,1)}) custom-call(s32[26,128]{1,0:T(8,128)} %bitcast.16, s32[26,128]{1,0:T(8,128)} %bitcast.17, s32[208,128]{1,0:T(8,128)} %bitcast.15, s32[1,128]{1,0:T(1,128)} %bitcast.18, f32[1,128]{1,0:T(1,128)} %bitcast.19, bf16[128,128]{1,0:T(8,128)(2,1)} %dense_ref.1, ...), custom_call_target="tpu_custom_call" | custom-call | tf_op jit(solution)/shard_map/pallas_call | solution.py:478
  183.8 1.4 slice_bitcast_fusion
  185.2 2.3 %copy.20 = f32[2048,128]{1,0:T(8,128)} copy(f32[2048,128]{1,0:T(8,128)} %get-tuple-element.16) | data formatting | bytes 2097152
  187.4 1.4 copy.21

commit v2 on v1

--- a/solution.py
+++ b/solution.py
@@ -11,8 +11,10 @@
 F32 = jnp.float32
 BF16 = jnp.bfloat16
 I32 = jnp.int32
+I16 = jnp.int16
 NT = (((1,), (1,)), ((), ()))
-LAG = 2
+LAG = 3
+UNROLL = 4
 
 
 def iota(shape, dim):
@@ -20,7 +22,19 @@
 
 
 def hot(mask):
-    return jnp.where(mask, 1.0, 0.0).astype(BF16)
+    return jnp.where(mask, jnp.ones((), BF16), jnp.zeros((), BF16))
+
+
+def wide(row):
+    return jnp.broadcast_to(row, (16, row.shape[1])).astype(I16)
+
+
+def hot_rows(index, row):
+    rows, lanes = index.shape[0], row.shape[1]
+    parts = []
+    for a in range(0, lanes, 128):
+        parts.append(hot(index.reshape(rows // 16, 16, 128) == wide(row[:, a:a + 128])[None]).reshape(rows, 128))
+    return jnp.concatenate(parts, axis=1) if len(parts) > 1 else parts[0]
 
 
 def kernel(
@@ -28,8 +42,8 @@
     own_ref, len_ref, rows_ref, label_ref, weight_ref, dense_ref, table_ref, bias_ref, head_ref,
     down_any, up_any,
     rg_ref, hb_ref, dg_ref,
-    down, up, pos_row, pos_col, req_acc, code_s, code_r, counts, pool_s, pool_r, grad_s, grad_r,
-    x0, x0_acc, cross, d_pool, chunk_acc, acc, pair_r, rs_r,
+    down, up, pos_row, slot_row, pos_col, owners, pick, turned_pick, req_acc, code_s, code_r, counts, pool_s, pool_r, grad_s, grad_r,
+    x0, x0_acc, cross, d_pool, acc, pair_r, rs_r,
     hb, h1, h2, h3, h4,
     w_sem, code_ss, code_rs, pool_ss, pool_rs, grad_ss, grad_rs,
     pr_ss, pr_rs, rs_ss, rs_rs, ag_ss, ag_rs, pa_ss, pa_rs, h_ss, h_rs,
@@ -89,34 +103,53 @@
     loop(1, pairs, lambda d: pl.semaphore_signal(barrier, inc=1, device_id=along_y(d), device_id_type=MESH))
     pl.semaphore_signal(barrier, inc=1, device_id=mate, device_id_type=MESH)
 
-    req_acc[...] = jnp.zeros_like(req_acc)
-    upper = jnp.concatenate([hot(iota((128, 128), 0) < iota((128, 128), 1)), jnp.ones((128, 128), BF16)], axis=1)
+    number = iota((max(chunk, 256), 128), 0).astype(I16)
+    lane = iota((16, 128), 1).astype(I16)
+    upper = jnp.concatenate(
+        [
+            jnp.where(iota((128, 128), 0) < iota((128, 128), 1), 1.0, 0.0).astype(BF16),
+            jnp.ones((128, 128), BF16),
+        ],
+        axis=1,
+    )
+    half = tables // 2
+    names = slots * 8
 
     def bucket(t, carry):
         owner = own_ref[pl.ds(t, 1), :]
         dx = ((owner >> bits) - x) & (ring - 1)
         dz = ((owner & (ring - 1)) - z) & (ring - 1)
         kind = ((dz - dx) & (ring - 1)) * ring + dx
-        mine = iota((128, 128), 0) == kind
-        mine_f = jnp.where(mine, 1.0, 0.0)
-        sums = jnp.dot(mine_f.astype(BF16), upper, preferred_element_type=F32)
-        slot = jnp.sum(mine_f * (sums[:, :128] + carry), axis=0, keepdims=True).astype(I32)
+        mine = jnp.where(iota((128, 128), 0) == kind, 1.0, 0.0)
+        mine_b = mine.astype(BF16)
+        owners[t // half, :, pl.ds(pl.multiple_of(lax.rem(t, half) * 128, 128), 128)] = mine_b
+        sums = jnp.dot(mine_b, upper, preferred_element_type=F32)
+        slot = jnp.sum(mine * (sums[:, :128] + carry), axis=0, keepdims=True).astype(I32)
         pos_row[pl.ds(t, 1), :] = kind * slots + slot
+        slot_row[pl.ds(t, 1), :] = slot
+        return carry + sums[:, 128:]
+
+    lax.fori_loop(0, tables, bucket, jnp.zeros((128, 128), F32), unroll=2)
+
+    def spread(t):
+        slot = slot_row[pl.ds(t, 1), :]
         live = iota((8, 128), 0) < len_ref[pl.ds(t, 1), :]
         code = jnp.where(live, rows_ref[pl.ds(pl.multiple_of(t * 8, 8), 8), :] + 1, 0)
-        high = (code >> 4).astype(F32)
-        low = (code & 15).astype(F32)
-        here = [slot == s for s in range(slots)]
-        spread = jnp.concatenate(
-            [jnp.where(h, high, 0.0) for h in here] + [jnp.where(h, low, 0.0) for h in here], axis=0
-        ).astype(BF16)
-        req_acc[...] += lax.dot_general(spread, mine_f.astype(BF16), NT, preferred_element_type=F32)
-        return carry + sums[:, 128:]
-
-    lax.fori_loop(0, tables, bucket, jnp.zeros((128, 128), F32))
+        here = iota((slots, 8, 128), 0) == slot[None]
+        top = pl.multiple_of((t // half) * 2 * names, 16)
+        lanes = pl.ds(pl.multiple_of(lax.rem(t, half) * 128, 128), 128)
+        for part, at in ((code >> 4, 0), (code & 15, names)):
+            value = jnp.where(here, part.astype(F32)[None], 0.0).reshape(names, 128).astype(BF16)
+            counts[pl.ds(top + at, names), lanes] = value
+
+    loop(0, tables, spread)
+    req = lax.dot_general(counts[0:2 * names, 0:half * 128], owners[0], NT, preferred_element_type=F32)
+    req_acc[...] = req
+    req = lax.dot_general(counts[2 * names:4 * names, 0:half * 128], owners[1], NT, preferred_element_type=F32)
+    req_acc[...] += req
     for p in range(code_rows):
         high = req_acc[p * 128:(p + 1) * 128, :]
-        low = req_acc[slots * 8 + p * 128:slots * 8 + (p + 1) * 128, :]
+        low = req_acc[names + p * 128:names + (p + 1) * 128, :]
         tile = (high * 16.0 + low - 1.0).T
         code_s[pl.ds(p, peers, stride=8), :] = tile[:peers].astype(I32)
 
@@ -139,7 +172,7 @@
 
     def turn(t):
         row = jnp.broadcast_to(pos_row[pl.ds(t, 1), :], (128, 128)).astype(F32)
-        pos_col[pl.ds(pl.multiple_of(t * 128, 128), 128), :] = row.T.astype(I32)
+        pos_col[pl.ds(pl.multiple_of(t * 128, 128), 128), :] = row.T.astype(I32).astype(I16)
         x0_acc[pl.ds(pl.multiple_of(t * 128, 128), 128), :] = jnp.zeros((128, 128), F32)
 
     loop(0, tables, turn)
@@ -155,23 +188,26 @@
             lanes = bags * 8
             spans = local_rows // 256
             key = (code >> 8) * bags + (iota((1, lanes), 1) >> 3)
-            left = hot(iota((spans * bags, lanes), 0) == key)
-            right = hot(iota((256, lanes), 0) == (code & 255))
+            left = hot_rows(number[:spans * bags], key)
+            right = hot_rows(number[:256], code & 255)
             out = lax.dot_general(left, right, NT, preferred_element_type=F32).astype(BF16)
             for s in range(spans):
                 counts[pl.ds(base + first * 16, bags), s * 256:(s + 1) * 256] = out[s * bags:(s + 1) * bags, :]
 
     def pool_chunk(j):
-        def one(i):
-            k = j * ring + i
-
-            @pl.when(k != 0)
+        def one(n):
+            first = j * ring + n * UNROLL
+
+            @pl.when(first != 0)
             def _():
-                code_copy(k).wait_recv()
-
-            count_bags(k)
-
-        loop(0, ring, one)
+                code_copy(first).wait_recv()
+
+            for i in range(1, UNROLL):
+                code_copy(first + i).wait_recv()
+            for i in range(UNROLL):
+                count_bags(first + i)
+
+        loop(0, ring // UNROLL, one)
         part = pl.ds(pl.multiple_of(j * chunk, 16), chunk)
         pool_s[part, :] = jnp.dot(counts[part, :], table_ref[...], preferred_element_type=F32).astype(BF16)
 
@@ -188,34 +224,46 @@
         def _():
             pool_r[0:slots, :] = pool_s[0:slots, :]
 
-    def place_chunk(j):
+    def place_pair(j):
         def one(i):
-            k = j * ring + i
+            k = j * 2 * ring + i
 
             @pl.when(k != 0)
             def _():
                 pool_copy(k).wait_recv()
 
-        loop(0, ring, one)
-        part = pl.ds(pl.multiple_of(j * chunk, 16), chunk)
+        loop(0, 2 * ring, one)
+        base = pl.multiple_of(j * 2 * chunk, 16)
+        offset = base.astype(I16)
 
         def some(t):
             rows = pl.ds(pl.multiple_of(t * 256, 256), 256)
-            column = pos_col[rows, :] - j * chunk
-            pick = jnp.concatenate([hot(column == iota((256, 128), 1) + q) for q in range(0, chunk, 128)], axis=1)
-            x0_acc[rows, :] += jnp.dot(pick, pool_r[part, :], preferred_element_type=F32)
+            column = (pos_col[rows, :] - offset).reshape(16, 16, 128)
+            column = jnp.where(column >= chunk, column - chunk, column)
+            for q in range(0, chunk, 128):
+                pick[rows, q:q + 128] = hot(column == (lane + q)[None]).reshape(256, 128)
 
         loop(0, tables // 2, some)
+        right = jnp.concatenate([pool_r[pl.ds(base, chunk), :], pool_r[pl.ds(base + chunk, chunk), :]], axis=1)
+
+        def apply(n):
+            rows = pl.ds(pl.multiple_of(n * half * 128, 128), half * 128)
+            out = jnp.dot(pick[rows, :], right, preferred_element_type=F32)
+            first = pos_col[rows, :].astype(I32) < base + chunk
+            x0_acc[rows, :] += jnp.where(first, out[:, :width], out[:, width:])
+
+        loop(0, 2, apply)
 
     def forward(j):
         pool_chunk(j)
-
-        @pl.when(j >= LAG)
-        def _():
-            place_chunk(j - LAG)
+        if ring >= 8:
+
+            @pl.when((j >= 5) & (lax.rem(j, 2) == 1))
+            def _():
+                place_pair((j - 5) // 2)
 
     loop(0, ring, forward)
-    loop(ring - LAG, ring, place_chunk)
+    loop(ring // 2 - 2 if ring >= 8 else 0, ring // 2, place_pair)
 
     down_copy.wait()
     up_copy.wait()
@@ -224,16 +272,13 @@
         x0[:, (t + 1) * width:(t + 2) * width] = x0_acc[t * 128:(t + 1) * 128, :].astype(BF16)
     step = 3 * width
     cuts = range(0, tiles * width, step)
-    low = jnp.zeros((128, down.shape[1]), F32)
-    for a in cuts:
-        low = low + jnp.dot(x0[:, a:a + step], down[a:a + step, :], preferred_element_type=F32)
-    low = low.astype(BF16)
+    low = jnp.dot(x0[...], down[...], preferred_element_type=F32).astype(BF16)
     logit_acc = jnp.zeros((128, width), F32)
     for a in cuts:
-        part = jnp.dot(low, up[:, a:a + step], preferred_element_type=F32) + bias_ref[:, a:a + step]
+        part = jnp.dot(low, up[:, a:a + step], preferred_element_type=F32) + bias_ref[a:a + step].reshape(1, step)
         cross[:, a:a + step] = part
         x0f = x0[:, a:a + step].astype(F32)
-        term = (x0f * part + x0f) * head_ref[:, a:a + step]
+        term = (x0f * part + x0f) * head_ref[a:a + step].reshape(1, step)
         for b in range(0, step, width):
             logit_acc = logit_acc + term[:, b:b + width]
     logit = jnp.sum(logit_acc, axis=1, keepdims=True)
@@ -241,19 +286,18 @@
     weight = jnp.broadcast_to(weight_ref[...], (128, 128)).T[:, 0:1]
     dlogit = weight * (jax.nn.sigmoid(logit) - label)
     hb[...] = jnp.zeros_like(hb)
-    d_low = jnp.zeros((128, down.shape[1]), F32)
     for a in cuts:
         x0f = x0[:, a:a + step].astype(F32)
         x1 = x0f * cross[:, a:a + step] + x0f
-        d_cross = dlogit * head_ref[:, a:a + step] * x0f
+        d_cross = dlogit * head_ref[a:a + step].reshape(1, step) * x0f
         head_part = jnp.sum(dlogit * x1, axis=0, keepdims=True)
         bias_part = jnp.sum(d_cross, axis=0, keepdims=True)
         for b in range(0, step, width):
             r = (a + b) // width
             hb[r:r + 1, :] = head_part[:, b:b + width]
             hb[tiles + r:tiles + r + 1, :] = bias_part[:, b:b + width]
-        d_low = d_low + lax.dot_general(d_cross.astype(BF16), up[:, a:a + step], NT, preferred_element_type=F32)
-    d_low = d_low.astype(BF16)
+        x0[:, a:a + step] = d_cross.astype(BF16)
+    d_low = lax.dot_general(x0[...], up[...], NT, preferred_element_type=F32).astype(BF16)
 
     def h_part(r):
         return pl.ds(pl.multiple_of(r * 8, 8), 8)
@@ -302,7 +346,7 @@
         loop(1, ring, lambda d: h5_copy(d).start())
 
     for a in cuts:
-        d_x1 = dlogit * head_ref[:, a:a + step]
+        d_x1 = dlogit * head_ref[a:a + step].reshape(1, step)
         d_x0 = d_x1 * (cross[:, a:a + step] + 1.0) + lax.dot_general(
             d_low, down[a:a + step, :], NT, preferred_element_type=F32
         )
@@ -315,21 +359,14 @@
                 d_pool[t * 128:(t + 1) * 128, :] = d_x0[:, b:b + width]
 
     def grad_chunk(j):
-        chunk_acc[...] = jnp.zeros_like(chunk_acc)
-
         def some(t):
-            rows = pl.ds(pl.multiple_of(t * 256, 256), 256)
-            pick = jnp.concatenate(
-                [
-                    hot(iota((chunk, 128), 0) == pos_row[pl.ds(t * 2 + h, 1), :] - j * chunk)
-                    for h in range(2)
-                ],
-                axis=1,
-            )
-            chunk_acc[...] += jnp.dot(pick, d_pool[rows, :], preferred_element_type=F32)
+            for h in range(2):
+                lanes = pl.ds(pl.multiple_of(t * 256 + h * 128, 128), 128)
+                turned_pick[:, lanes] = hot_rows(number[:chunk], pos_row[pl.ds(t * 2 + h, 1), :] - j * chunk)
 
         loop(0, tables // 2, some)
-        grad_s[pl.ds(pl.multiple_of(j * chunk, 16), chunk), :] = chunk_acc[...].astype(BF16)
+        out = jnp.dot(turned_pick[...], d_pool[...], preferred_element_type=F32)
+        grad_s[pl.ds(pl.multiple_of(j * chunk, 16), chunk), :] = out.astype(BF16)
 
         def send(i):
             k = j * ring + i
@@ -355,10 +392,11 @@
         loop(0, ring, one)
         part = pl.ds(pl.multiple_of(j * chunk, 16), chunk)
         turned = grad_r[part, :].astype(F32).T.astype(BF16)
-        for b in range(groups):
-            acc[b] += jnp.dot(
-                turned, counts[part, b * block:(b + 1) * block], preferred_element_type=F32
-            )
+        for b in range(0, local_rows, 256):
+            out = jnp.dot(turned, counts[part, b:b + 256], preferred_element_type=F32)
+            for a in range(0, 256, 128):
+                g, at = (a + b) // block, (a + b) % block
+                acc[g, :, at:at + 128] += out[:, a:a + 128]
 
     def backward(j):
         grad_chunk(j)
@@ -488,11 +526,15 @@
             pltpu.VMEM((cross_width, rank), BF16),
             pltpu.VMEM((rank, cross_width), BF16),
             pltpu.VMEM((-(-tables // 8) * 8, 128), I32),
-            pltpu.VMEM((bags, 128), I32),
+            pltpu.VMEM((-(-tables // 8) * 8, 128), I32),
+            pltpu.VMEM((bags, 128), I16),
+            pltpu.VMEM((2, 128, bags // 2), BF16),
+            pltpu.VMEM((bags, chunk), BF16),
+            pltpu.VMEM((chunk, bags), BF16),
             pltpu.VMEM((2 * slots * 8, 128), F32),
             pltpu.VMEM((peers * 8, 128), I32),
             pltpu.VMEM((peers * 8, 128), I32),
-            pltpu.VMEM((peers * slots, local_rows), BF16),
+            pltpu.VMEM((max(peers, 32) * slots, local_rows), BF16),
             pltpu.VMEM((peers * slots, width), BF16),
             pltpu.VMEM((peers * slots, width), BF16),
             pltpu.VMEM((peers * slots, width), BF16),
@@ -501,7 +543,6 @@
             pltpu.VMEM((bags, width), F32),
             pltpu.VMEM((samples, cross_width), F32),
             pltpu.VMEM((bags, width), BF16),
-            pltpu.VMEM((chunk, width), F32),
             pltpu.VMEM((groups, width, block), F32),
             pltpu.VMEM((pairs, width, block), F32),
             pltpu.VMEM((pairs, width, block), F32),
@@ -533,7 +574,7 @@
         ),
     )(
         own, lengths, rows, labels.reshape(1, samples), sample_weight.reshape(1, samples), dense_part, table_window,
-        cross_bias.reshape(1, cross_width), head_w.reshape(1, cross_width), down_w, up_w,
+        cross_bias, head_w, down_w, up_w,
     )
     head_grad = sums[:tiles].reshape(cross_width)
     bias_grad = sums[tiles:2 * tiles].reshape(cross_width)

time: 190 us -> 166 us (0.87)
  Pallas kernels: 179 us -> 156 us
  local copies, waits for them, and re-layouts: 9.01 us -> 6.36 us
    pallas_call x1, Pallas kernels: 179 us -> 156 us  [body(): pl.pallas_call(functools.partial(kernel, ring, tables, slots, pairs), out...]
    reshape x2 -> x0, local copies, waits for them, and re-layouts: 2.65 us -> none  [the longest x1 1.33 us: body(): cross_bias.reshape(1, cross_width)]
where the time goes in v2:
time: 166 us; the launch traced here: 163 us
  Pallas kernels  156 us (94%)
  local copies, waits for them, and re-layouts  6.36 us (4%)
    pallas_call x1, Pallas kernels, body(): pl.pallas_call(functools.partial(kernel, ring, tables, slots, pairs), out...  156 us
    unnamed x3, local copies, waits for them, and re-layouts  4.95 us

profile of v2, /device:TPU:1, one launch (start us, length us, event | category | flops | bytes accessed | tf_op | source)
XLA Modules:
  0.0 163.5 jit_solution(16338003685149910985)
XLA Ops:
  0.6 1.3 copy.17
  1.9 156.5 %shard_map.138 = (f32[2048,128]{1,0:T(8,128)}, f32[64,128]{1,0:T(8,128)}, bf16[128,128]{1,0:T(8,128)(2,1)}) custom-call(s32[26,128]{1,0:T(8,128)} %bitcast.16, s32[26,128]{1,0:T(8,128)} %bitcast.17, s32[208,128]{1,0:T(8,128)} %bitcast.15, s32[1,128]{1,0:T(1,128)} %bitcast.18, f32[1,128]{1,0:T(1,128)} %bitcast.19, bf16[128,128]{1,0:T(8,128)(2,1)} %dense_ref.1, ...), custom_call_target="tpu_custom_call" | custom-call | tf_op jit(solution)/shard_map/pallas_call | solution.py:516
  158.5 1.4 slice_bitcast_fusion
  159.9 2.3 %copy.20 = f32[2048,128]{1,0:T(8,128)} copy(f32[2048,128]{1,0:T(8,128)} %get-tuple-element.16) | data formatting | bytes 2097152
  162.1 1.4 copy.21

commit v3 on v2

--- a/solution.py
+++ b/solution.py
@@ -43,7 +43,7 @@
     down_any, up_any,
     rg_ref, hb_ref, dg_ref,
     down, up, pos_row, slot_row, pos_col, owners, pick, turned_pick, req_acc, code_s, code_r, counts, pool_s, pool_r, grad_s, grad_r,
-    x0, x0_acc, cross, d_pool, acc, pair_r, rs_r,
+    x0, x0_acc, cross, d_pool, acc, pair_r, rs_s, rs_r,
     hb, h1, h2, h3, h4,
     w_sem, code_ss, code_rs, pool_ss, pool_rs, grad_ss, grad_rs,
     pr_ss, pr_rs, rs_ss, rs_rs, ag_ss, ag_rs, pa_ss, pa_rs, h_ss, h_rs,
@@ -156,7 +156,7 @@
     pl.semaphore_wait(barrier, peers - 1 + pairs - 1 + 1)
 
     def code_copy(k):
-        part = pl.ds(pl.multiple_of(k * 8, 8), 8)
+        part = pl.ds(pl.multiple_of(k * 8, 8), code_rows)
         return remote(code_s.at[part], code_r.at[part], code_ss.at[k], code_rs.at[k], ahead(k))
 
     def pool_copy(k):
@@ -175,8 +175,6 @@
         pos_col[pl.ds(pl.multiple_of(t * 128, 128), 128), :] = row.T.astype(I32).astype(I16)
         x0_acc[pl.ds(pl.multiple_of(t * 128, 128), 128), :] = jnp.zeros((128, 128), F32)
 
-    loop(0, tables, turn)
-    acc[...] = jnp.zeros_like(acc)
 
     def count_bags(k):
         tile = code_r[pl.ds(pl.multiple_of(k * 8, 8), 8), :]
@@ -256,6 +254,12 @@
 
     def forward(j):
         pool_chunk(j)
+
+        @pl.when(j == 1)
+        def _():
+            loop(0, tables, turn)
+            acc[...] = jnp.zeros_like(acc)
+
         if ring >= 8:
 
             @pl.when((j >= 5) & (lax.rem(j, 2) == 1))
@@ -415,7 +419,7 @@
         return remote(acc.at[(1 - c) * pairs + r], pair_r.at[r], pr_ss.at[d], pr_rs.at[d], mate)
 
     def rs_copy(d):
-        return remote(pair_r.at[lax.rem(y + d, pairs)], rs_r.at[d], rs_ss.at[d], rs_rs.at[d], along_y(d))
+        return remote(rs_s.at[lax.rem(y + d, pairs)], rs_r.at[d], rs_ss.at[d], rs_rs.at[d], along_y(d))
 
     def out_block(side, r):
         return rg_ref.at[pl.ds(pl.multiple_of((side * pairs + r) * block, block), block)]
@@ -434,7 +438,9 @@
         d = lax.rem(n + 1, pairs)
         pr_copy(d).wait_recv()
         r = lax.rem(y + d, pairs)
-        pair_r[r] = pair_r[r] + acc[c * pairs + r]
+        both = pair_r[r] + acc[c * pairs + r]
+        pair_r[r] = both
+        rs_s[r] = both.astype(BF16)
 
         @pl.when(d != 0)
         def _():
@@ -445,8 +451,8 @@
     loop(1, pairs, lambda d: rs_copy(d).wait_recv())
     total = pair_r[y]
     for d in range(1, pairs):
-        total = total + rs_r[d]
-    rg_ref[pl.ds(pl.multiple_of((c * pairs + y) * block, block), block), :] = total.T
+        total = total + rs_r[d].astype(F32)
+    rg_ref[pl.ds(pl.multiple_of((c * pairs + y) * block, block), block), :] = total.T.astype(BF16)
     loop(1, pairs, lambda d: ag_copy(d).start())
     pa_copy(0).start()
     h_step4()
@@ -516,7 +522,7 @@
     row_grad, sums, dense_grad = pl.pallas_call(
         functools.partial(kernel, ring, tables, slots, pairs),
         out_shape=(
-            jax.ShapeDtypeStruct((local_rows, width), F32),
+            jax.ShapeDtypeStruct((local_rows, width), BF16),
             jax.ShapeDtypeStruct((ring * 8, width), F32),
             jax.ShapeDtypeStruct((samples, width), BF16),
         ),
@@ -545,7 +551,8 @@
             pltpu.VMEM((bags, width), BF16),
             pltpu.VMEM((groups, width, block), F32),
             pltpu.VMEM((pairs, width, block), F32),
-            pltpu.VMEM((pairs, width, block), F32),
+            pltpu.VMEM((pairs, width, block), BF16),
+            pltpu.VMEM((pairs, width, block), BF16),
             pltpu.VMEM((ring * 8, 128), F32),
             pltpu.VMEM((ring * 8, 128), F32),
             pltpu.VMEM((ring * 8, 128), F32),
@@ -578,7 +585,7 @@
     )
     head_grad = sums[:tiles].reshape(cross_width)
     bias_grad = sums[tiles:2 * tiles].reshape(cross_width)
-    return row_grad, head_grad, bias_grad, dense_grad
+    return row_grad.astype(F32), head_grad, bias_grad, dense_grad
 
 
 def solution(mesh):

time: 166 us -> 156 us (0.940)
  Pallas kernels: 156 us -> 147 us
  local copies, waits for them, and re-layouts: 6.36 us -> 4.1 us
  other arithmetic: 0 us -> 2.08 us
    pallas_call x1, Pallas kernels: 156 us -> 147 us  [body(): pl.pallas_call(functools.partial(kernel, ring, tables, slots, pairs), out...]
    unnamed x3 -> x2, local copies, waits for them, and re-layouts: 4.95 us -> 2.69 us
    convert_element_type x0 -> x1, other arithmetic: none -> 2.08 us  [body(): return (row_grad.astype(F32), head_grad, bias_grad, dense_grad)]
where the time goes in v3:
time: 156 us; the launch traced here: 154 us
  Pallas kernels  147 us (94%)
  local copies, waits for them, and re-layouts  4.1 us (3%)
  other arithmetic  2.08 us (1%)
    pallas_call x1, Pallas kernels, body(): pl.pallas_call(functools.partial(kernel, ring, tables, slots, pairs), out...  147 us

profile of v3, /device:TPU:1, one launch (start us, length us, event | category | flops | bytes accessed | tf_op | source)
XLA Modules:
  0.0 153.6 jit_solution(16992308121282078393)
XLA Ops:
  0.6 1.3 copy.17
  1.9 146.8 %shard_map.138 = (bf16[2048,128]{1,0:T(8,128)(2,1)}, f32[64,128]{1,0:T(8,128)}, bf16[128,128]{1,0:T(8,128)(2,1)}) custom-call(s32[26,128]{1,0:T(8,128)} %bitcast.16, s32[26,128]{1,0:T(8,128)} %bitcast.17, s32[208,128]{1,0:T(8,128)} %bitcast.15, s32[1,128]{1,0:T(1,128)} %bitcast.18, f32[1,128]{1,0:T(1,128)} %bitcast.19, bf16[128,128]{1,0:T(8,128)(2,1)} %dense_ref.1, ...), custom_call_target="tpu_custom_call" | custom-call | tf_op jit(solution)/shard_map/pallas_call | solution.py:522
  148.7 1.4 slice_bitcast_fusion
  150.2 2.1 %convert_element_type.3 = f32[2048,128]{1,0:T(8,128)} convert(bf16[2048,128]{1,0:T(8,128)(2,1)} %get-tuple-element.7) | non-fusion elementwise | flops 262144 | bytes 1572864 | tf_op jit(solution)/shard_map/convert_element_type | solution.py:588
  152.2 1.4 copy.19

commit v4 on v3

--- a/solution.py
+++ b/solution.py
@@ -63,13 +63,13 @@
     mate = {"grp": grp + 1 - 2 * c}
 
     def ahead(k):
-        dx = lax.rem(k, ring)
-        dz = lax.rem(dx + k // ring, ring)
+        dx = lax.rem(3 * k, ring)
+        dz = lax.rem(3 * (k // ring) + ring - dx, ring)
         return {"emb": lax.rem(x + dx, ring) * ring + lax.rem(z + dz, ring)}
 
     def behind(k):
-        dx = lax.rem(k, ring)
-        dz = lax.rem(dx + k // ring, ring)
+        dx = lax.rem(3 * k, ring)
+        dz = lax.rem(3 * (k // ring) + ring - dx, ring)
         return {"emb": lax.rem(x + ring - dx, ring) * ring + lax.rem(z + ring - dz, ring)}
 
     def along_x(d):
@@ -119,7 +119,7 @@
         owner = own_ref[pl.ds(t, 1), :]
         dx = ((owner >> bits) - x) & (ring - 1)
         dz = ((owner & (ring - 1)) - z) & (ring - 1)
-        kind = ((dz - dx) & (ring - 1)) * ring + dx
+        kind = ((3 * (dz + dx)) & (ring - 1)) * ring + ((3 * dx) & (ring - 1))
         mine = jnp.where(iota((128, 128), 0) == kind, 1.0, 0.0)
         mine_b = mine.astype(BF16)
         owners[t // half, :, pl.ds(pl.multiple_of(lax.rem(t, half) * 128, 128), 128)] = mine_b

time: 156 us -> 152 us (0.974)
  Pallas kernels: 147 us -> 144 us
    pallas_call x1, Pallas kernels: 147 us -> 144 us  [body(): pl.pallas_call(functools.partial(kernel, ring, tables, slots, pairs), out...]
where the time goes in v4:
time: 152 us; the launch traced here: 151 us
  Pallas kernels  144 us (95%)
  local copies, waits for them, and re-layouts  4.1 us (3%)
  other arithmetic  2.08 us (1%)
    pallas_call x1, Pallas kernels, body(): pl.pallas_call(functools.partial(kernel, ring, tables, slots, pairs), out...  144 us

profile of v4, /device:TPU:1, one launch (start us, length us, event | category | flops | bytes accessed | tf_op | source)
XLA Modules:
  0.0 151.1 jit_solution(17234432532587634373)
XLA Ops:
  0.6 1.3 copy.17
  1.9 144.3 %shard_map.138 = (bf16[2048,128]{1,0:T(8,128)(2,1)}, f32[64,128]{1,0:T(8,128)}, bf16[128,128]{1,0:T(8,128)(2,1)}) custom-call(s32[26,128]{1,0:T(8,128)} %bitcast.16, s32[26,128]{1,0:T(8,128)} %bitcast.17, s32[208,128]{1,0:T(8,128)} %bitcast.15, s32[1,128]{1,0:T(1,128)} %bitcast.18, f32[1,128]{1,0:T(1,128)} %bitcast.19, bf16[128,128]{1,0:T(8,128)(2,1)} %dense_ref.1, ...), custom_call_target="tpu_custom_call" | custom-call | tf_op jit(solution)/shard_map/pallas_call | solution.py:522
  146.3 1.4 slice_bitcast_fusion
  147.7 2.1 %convert_element_type.3 = f32[2048,128]{1,0:T(8,128)} convert(bf16[2048,128]{1,0:T(8,128)(2,1)} %get-tuple-element.7) | non-fusion elementwise | flops 262144 | bytes 1572864 | tf_op jit(solution)/shard_map/convert_element_type | solution.py:588
  149.8 1.4 copy.19
